TPU v7x, 512 devices: a whole 4x4x16 slice. The times are simulated.
512 devices in a mesh: dp: 32 (over y, x, core), tensor: 16 (over z).
Axes of the slice: x: 4, y: 4, z: 16, core: 2. Of those that a mesh axis runs over, the one named last changes fastest.
Arguments:
- attn_out: bfloat16 [3, 2048, 4096], P(None, 'dp', 'tensor'), may hold values from -6 to 6
- base_weight: bfloat16 [4096, 4096], P('tensor'), may hold values from -0.09375 to 0.09375
- store_a: bfloat16 [128, 4096, 128], P('dp', 'tensor'), may hold values from -0.09375 to 0.09375
- store_b: bfloat16 [128, 128, 4096], P('dp', None, 'tensor'), may hold values from -0.5 to 0.5
- adapter_lists: int32 [32, 16], P('dp'), may hold values from 0 to 127, as said below
- placement_map: int32 [128], replicated, may hold values from 0 to 127, as said below
- request_slot: int32 [2048], P('dp'), may hold values from 0 to 15
Outputs:
- projected: bfloat16 [3, 2048, 4096], P(None, 'dp', 'tensor')
Inputs may be any that keep to these rules, and one draw needn't show every extreme that they name: `adapter_lists`: each replica's 16 adapters are stored on 16 different indices of dp. `placement_map` is a permutation; adapter a's panels are row placement_map[a] of the stores, held by index placement_map[a] // 4 of dp.
All inputs are finite; a program needn't handle non-finite values.
Results may differ from a plain program's by a relative error of at most 0.001.
Values may be sent and summed in bfloat16 or wider, within the bound.
No kernel may reach another device: no remote copies, remote signals or barrier semaphores. Data moves between devices by JAX's collectives and lax.ppermute only.
A program may use at most 64 MiB of HBM per device.

v0:
```python
import jax
import jax.numpy as jnp
from jax import lax
from jax.sharding import PartitionSpec as P


def on_device(attn_out, base_weight, store_a, store_b, adapter_lists, placement_map, request_slot):
    replicas = lax.axis_size("dp")
    stored = store_a.shape[0]
    slot_count = adapter_lists.shape[1]
    rank_width = store_a.shape[2]
    requests = request_slot.shape[0]
    catalog = placement_map.shape[0]
    my_list = adapter_lists[0]
    matches = my_list[:, None] == jnp.arange(catalog, dtype=jnp.int32)[None, :]
    position = jnp.sum(jnp.where(matches, placement_map[None, :], 0), axis=1)
    holder = position // stored
    local_slot = position % stored
    devices = jnp.arange(replicas, dtype=jnp.int32)
    wanted = (
        jnp.sum(jnp.where(holder[None, :] == devices[:, None], local_slot[None, :] + 1, 0), axis=1)
        - 1
    )
    every_wish = lax.all_gather(wanted[None, :], "dp", axis=0, tiled=True)
    own_index = lax.axis_index("dp")
    asked_slot = lax.dynamic_index_in_dim(every_wish, own_index, 1, keepdims=False)
    picker = (asked_slot[:, None] == jnp.arange(stored, dtype=jnp.int32)[None, :]).astype(
        jnp.bfloat16
    )
    slot_hit = (request_slot[:, None] == jnp.arange(slot_count, dtype=jnp.int32)[None, :]).astype(
        jnp.float32
    )
    step_results = []
    for step_index in range(attn_out.shape[0]):
        send_a = jnp.einsum(
            "qn,nir->qir", picker, store_a, preferred_element_type=jnp.float32
        ).astype(jnp.bfloat16)
        send_b = jnp.einsum(
            "qn,nro->qro", picker, store_b, preferred_element_type=jnp.float32
        ).astype(jnp.bfloat16)
        recv_a = lax.all_to_all(send_a, "dp", split_axis=0, concat_axis=0, tiled=True)
        recv_b = lax.all_to_all(send_b, "dp", split_axis=0, concat_axis=0, tiled=True)
        slot_a = jnp.take(recv_a, holder, axis=0)
        slot_b = jnp.take(recv_b, holder, axis=0)
        fetch_stack_a = jnp.transpose(slot_a, (1, 0, 2)).reshape(
            slot_a.shape[1], slot_count * rank_width
        )
        fetch_stack_b = slot_b.reshape(slot_count * rank_width, slot_b.shape[2]).astype(jnp.float32)
        step_in = attn_out[step_index]
        base_output_sum = lax.psum_scatter(
            lax.dot_general(
                base_weight, step_in, (((0,), (1,)), ((), ())), preferred_element_type=jnp.float32
            ),
            "tensor",
            scatter_dimension=0,
            tiled=True,
        )
        every_slot = jnp.dot(step_in, fetch_stack_a, preferred_element_type=jnp.float32).reshape(
            requests, slot_count, rank_width
        )
        rank_part = jnp.sum(every_slot * slot_hit[:, :, None], axis=1)
        rank_reduce = lax.psum(rank_part, "tensor")
        spread = (slot_hit[:, :, None] * rank_reduce[:, None, :]).reshape(
            requests, slot_count * rank_width
        )
        low_rank_delta = jnp.dot(
            spread,
            fetch_stack_b,
            precision=lax.Precision.HIGHEST,
            preferred_element_type=jnp.float32,
        )
        step_results.append((base_output_sum.T + low_rank_delta).astype(jnp.bfloat16))
    return jnp.stack(step_results)


def solution(mesh):
    placed = (
        P(None, "dp", "tensor"),
        P("tensor", None),
        P("dp", "tensor", None),
        P("dp", None, "tensor"),
        P("dp", None),
        P(),
        P("dp"),
    )
    return jax.shard_map(
        on_device, mesh=mesh, in_specs=placed, out_specs=P(None, "dp", "tensor"), check_vma=False
    )
```

profile of v0, /device:TPU:8, one launch (start us, length us, event | category | flops | bytes accessed | tf_op | source)
XLA Modules:
  0.0 509.3 jit_solution(18405111244604827407)
XLA Ops:
  6.5 1.0 select_reduce_fusion.1
  7.7 1.3 dynamic-slice
  9.8 111.4 %all-reduce.1 = s32[32,32]{1,0:T(8,128)S(1)} all-reduce(s32[32,32]{1,0:T(8,128)S(1)} %reshape.118), channel_id=2, replica_groups=mesh['dp'=32,'tensor'=16] {'dp'}, use_global_device_ids=true, to_apply=%add | all-reduce | flops 1024 | bytes 8192
  121.3 1.7 convolution_convert_fusion.1
  123.1 2.1 copy.40
  125.2 22.7 %all-to-all-start = ((bf16[32,256,128]{2,1,0:T(8,128)(2,1)}), bf16[32,256,128]{2,1,0:T(8,128)(2,1)}, u32[]{:S(2)}, u32[]{:S(2)}) async-start(bf16[32,256,128]{2,1,0:T(8,128)(2,1)} %copy.40), calls=%async_computation.1 | async-start | bytes 4194304 | tf_op jit(solution)/shard_map/all_to_all | solution.py:41
  148.0 1.5 fusion.30
  149.6 24.9 %all-to-all-done = bf16[32,256,128]{2,1,0:T(8,128)(2,1)} async-done(((bf16[32,256,128]{2,1,0:T(8,128)(2,1)}), bf16[32,256,128]{2,1,0:T(8,128)(2,1)}, u32[]{:S(2)}, u32[]{:S(2)}) %all-to-all-start) | async-done | bytes 2097184 | tf_op jit(solution)/shard_map/all_to_all | solution.py:41
  174.5 2.3 gather_fusion
  176.9 1.2 select_bitcast_fusion
  178.0 1.5 copy.41
  181.7 1.5 fusion.27
  184.0 2.5 copy.44
  186.5 8.1 %all-to-all-start.1 = ((bf16[32,128,256]{2,1,0:T(8,128)(2,1)}), bf16[32,128,256]{2,1,0:T(8,128)(2,1)}, u32[]{:S(2)}, u32[]{:S(2)}) async-start(bf16[32,128,256]{2,1,0:T(8,128)(2,1)} %copy.44), calls=%async_computation.2 | async-start | bytes 4194304 | tf_op jit(solution)/shard_map/all_to_all | solution.py:42
  194.7 1.5 fusion.24
  196.3 25.0 %all-to-all-done.1 = bf16[32,128,256]{2,1,0:T(8,128)(2,1)} async-done(((bf16[32,128,256]{2,1,0:T(8,128)(2,1)}), bf16[32,128,256]{2,1,0:T(8,128)(2,1)}, u32[]{:S(2)}, u32[]{:S(2)}) %all-to-all-start.1) | async-done | bytes 2097184 | tf_op jit(solution)/shard_map/all_to_all | solution.py:42
  221.3 2.2 gather_fusion.1
  223.5 2.1 reduce-scatter.4.cloned.1.call-done
  225.6 134.7 %all-reduce.5.cloned.1.call-done = (f32[64,128]{1,0:T(8,128)}, f32[64,128]{1,0:T(8,128)}, f32[64,128]{1,0:T(8,128)}) async-done(((f32[64,128]{1,0:T(8,128)}, f32[64,128]{1,0:T(8,128)}, f32[64,128]{1,0:T(8,128)}), (f32[64,128]{1,0:T(8,128)}, f32[64,128]{1,0:T(8,128)}, f32[64,128]{1,0:T(8,128)})) %all-reduce.5.cloned.1.call-update) | async-done | bytes 98320 | tf_op jit(solution)/shard_map/psum | solution.py:62
  360.3 1.6 fusion.6
  361.9 67.5 %reduce-scatter.6.cloned.1.call-done = f32[256,64]{0,1:T(8,128)} async-done(((f32[4096,64]{0,1:T(8,128)}), f32[256,64]{0,1:T(8,128)}) %reduce-scatter.6.cloned.1.call-update) | async-done | bytes 65552 | tf_op jit(solution)/shard_map/reduce_scatter | solution.py:50
  429.4 1.6 fusion.7
  431.0 69.5 %reduce-scatter.8.cloned.1.call-done = f32[256,64]{0,1:T(8,128)} async-done(((f32[4096,64]{0,1:T(8,128)}), f32[256,64]{0,1:T(8,128)}) %reduce-scatter.8.cloned.1.call-update) | async-done | bytes 65552 | tf_op jit(solution)/shard_map/reduce_scatter | solution.py:50
  500.5 1.6 fusion.8
  (34 shorter events, 4.3 us)
Async XLA Ops:
  6.5 141.5 %copy-start = (bf16[256,4096]{1,0:T(8,128)(2,1)S(1)}, bf16[256,4096]{1,0:T(8,128)(2,1)}, u32[]{:S(2)}) copy-start(bf16[256,4096]{1,0:T(8,128)(2,1)} %param.12) | copy-start | bytes 6291460
  125.2 22.8 %copy-start.1 = (bf16[3,64,256]{2,1,0:T(8,128)(2,1)S(1)}, bf16[3,64,256]{2,1,0:T(8,128)(2,1)}, u32[]{:S(2)}) copy-start(bf16[3,64,256]{2,1,0:T(8,128)(2,1)} %param.11) | copy-start | bytes 294916
  125.2 49.3 %all-to-all-start = ((bf16[32,256,128]{2,1,0:T(8,128)(2,1)}), bf16[32,256,128]{2,1,0:T(8,128)(2,1)}, u32[]{:S(2)}, u32[]{:S(2)}) async-start(bf16[32,256,128]{2,1,0:T(8,128)(2,1)} %copy.40), calls=%async_computation.1 | async-start | bytes 4194304 | tf_op jit(solution)/shard_map/all_to_all | solution.py:41
  147.9 1.6 copy-start.3
  147.9 77.7 %reduce-scatter.4.cloned.1.call-start = ((), (), s32[]{:S(2)}) async-start(), calls=%async_computation.5 | async-start | bytes 1114112 | tf_op jit(solution)/shard_map/reduce_scatter | solution.py:50
  149.5 210.8 %all-reduce.5.cloned.1.call-start = ((), (), s32[]{:S(2)}) async-start(), calls=%async_computation.8 | async-start | bytes 196608 | tf_op jit(solution)/shard_map/psum | solution.py:62
  181.7 1.6 copy-start.2
  181.7 247.7 %reduce-scatter.6.cloned.1.call-start = ((), (), s32[]{:S(2)}) async-start(), calls=%async_computation.6 | async-start | bytes 1114112 | tf_op jit(solution)/shard_map/reduce_scatter | solution.py:50
  186.5 34.7 %all-to-all-start.1 = ((bf16[32,128,256]{2,1,0:T(8,128)(2,1)}), bf16[32,128,256]{2,1,0:T(8,128)(2,1)}, u32[]{:S(2)}, u32[]{:S(2)}) async-start(bf16[32,128,256]{2,1,0:T(8,128)(2,1)} %copy.44), calls=%async_computation.2 | async-start | bytes 4194304 | tf_op jit(solution)/shard_map/all_to_all | solution.py:42
  194.7 305.9 %reduce-scatter.8.cloned.1.call-start = ((), (), s32[]{:S(2)}) async-start(), calls=%async_computation.7 | async-start | bytes 1114112 | tf_op jit(solution)/shard_map/reduce_scatter | solution.py:50
  360.3 140.2 %copy-start.4 = (f32[64,128]{1,0:T(8,128)S(1)}, f32[64,128]{1,0:T(8,128)}, u32[]{:S(2)}) copy-start(f32[64,128]{1,0:T(8,128)} %get-tuple-element.10) | copy-start | bytes 98308
Sparse Core Ops, SparseCore 0:
  151.6 73.9 reduce-scatter.3
  228.3 131.9 all-reduce.4
  363.1 66.2 reduce-scatter.5
  432.3 68.1 reduce-scatter.7
where the time goes:
time: 510 us; the launch traced here: 509 us
  waiting for transfers between devices  324 us (64%)
  blocking collectives  111 us (22%)
  starting transfers between devices  31.1 us (6%)
  between operations  13.9 us (3%)
  matrix products  13.1 us (3%)
  local copies, waits for them, and re-layouts  12.2 us (2%)
    reduce_scatter x3, waiting for transfers between devices, on_device(): lax.psum_scatter(lax.dot_general(base_weight, step_in, (((0,), (1,)), (()...  139 us
    psum x1, waiting for transfers between devices, on_device(): rank_reduce = lax.psum(rank_part, 'tensor')  135 us
    unnamed x1, blocking collectives  111 us
    all_to_all x1, waiting for transfers between devices, on_device(): lax.all_to_all(send_b, 'dp', split_axis=0, concat_axis=0, tiled=True)  25 us
    all_to_all x1, waiting for transfers between devices, on_device(): lax.all_to_all(send_a, 'dp', split_axis=0, concat_axis=0, tiled=True)  24.9 us
    all_to_all x1, starting transfers between devices, on_device(): lax.all_to_all(send_a, 'dp', split_axis=0, concat_axis=0, tiled=True)  22.7 us
  transfers between devices with their start and end apart: 6, of which 6 were waited for; matrix products, arithmetic and copies ran while one was open for 4% of the time, Pallas kernels for 0%

commit v1 on v0

--- a/solution.py
+++ b/solution.py
@@ -2,6 +2,12 @@
 import jax.numpy as jnp
 from jax import lax
 from jax.sharding import PartitionSpec as P
+
+
+def add_all(x, mesh_axis):
+    parts = lax.all_gather(x, mesh_axis, axis=0, tiled=False)
+    total = parts.sum(axis=0)
+    return total
 
 
 def on_device(attn_out, base_weight, store_a, store_b, adapter_lists, placement_map, request_slot):
@@ -59,7 +65,7 @@
             requests, slot_count, rank_width
         )
         rank_part = jnp.sum(every_slot * slot_hit[:, :, None], axis=1)
-        rank_reduce = lax.psum(rank_part, "tensor")
+        rank_reduce = add_all(rank_part, "tensor")
         spread = (slot_hit[:, :, None] * rank_reduce[:, None, :]).reshape(
             requests, slot_count * rank_width
         )

time: 510 us -> 307 us (0.60)
  the two profiles are of different devices: /device:TPU:8 before, /device:TPU:10 now
where the time goes in v1:
time: 307 us; the launch traced here: 306 us
  blocking collectives  205 us (67%)
  starting transfers between devices  36.9 us (12%)
  waiting for transfers between devices  20.8 us (7%)
  between operations  14 us (5%)
  local copies, waits for them, and re-layouts  13.8 us (4%)
  matrix products  12.9 us (4%)
    unnamed x1, blocking collectives  106 us
    all_gather x3, blocking collectives, add_all(): parts = lax.all_gather(x, mesh_axis, axis=0, tiled=False)  98.9 us
    all_to_all x1, starting transfers between devices, on_device(): lax.all_to_all(send_a, 'dp', split_axis=0, concat_axis=0, tiled=True)  27.6 us
    all_to_all x1, waiting for transfers between devices, on_device(): lax.all_to_all(send_a, 'dp', split_axis=0, concat_axis=0, tiled=True)  20.7 us
    all_to_all x1, starting transfers between devices, on_device(): lax.all_to_all(send_b, 'dp', split_axis=0, concat_axis=0, tiled=True)  9.14 us
  transfers between devices with their start and end apart: 5, of which 1 were waited for; matrix products, arithmetic and copies ran while one was open for 8% of the time, Pallas kernels for 0%

profile of v1, /device:TPU:10, one launch (start us, length us, event | category | flops | bytes accessed | tf_op | source)
XLA Modules:
  0.0 306.1 jit_solution(10289947724386621342)
XLA Ops:
  6.5 1.6 copy-done
  8.1 2.2 fusion.30
  10.5 1.5 fusion.27
  12.3 1.3 dynamic-slice
  14.4 106.3 %all-reduce.1 = s32[32,32]{1,0:T(8,128)S(1)} all-reduce(s32[32,32]{1,0:T(8,128)S(1)} %reshape.118), channel_id=2, replica_groups=mesh['dp'=32,'tensor'=16] {'dp'}, use_global_device_ids=true, to_apply=%add | all-reduce | flops 1024 | bytes 8192
  120.9 0.8 convolution_convert_fusion.1
  121.7 2.1 copy.40
  123.8 27.6 %all-to-all-start = ((bf16[32,256,128]{2,1,0:T(8,128)(2,1)}), bf16[32,256,128]{2,1,0:T(8,128)(2,1)}, u32[]{:S(2)}, u32[]{:S(2)}) async-start(bf16[32,256,128]{2,1,0:T(8,128)(2,1)} %copy.40), calls=%async_computation.1 | async-start | bytes 4194304 | tf_op jit(solution)/shard_map/all_to_all | solution.py:47
  151.6 1.6 fusion.24
  153.2 0.8 convolution_convert_fusion
  153.9 2.5 copy.44
  156.4 20.7 %all-to-all-done = bf16[32,256,128]{2,1,0:T(8,128)(2,1)} async-done(((bf16[32,256,128]{2,1,0:T(8,128)(2,1)}), bf16[32,256,128]{2,1,0:T(8,128)(2,1)}, u32[]{:S(2)}, u32[]{:S(2)}) %all-to-all-start) | async-done | bytes 2097184 | tf_op jit(solution)/shard_map/all_to_all | solution.py:47
  177.1 9.1 %all-to-all-start.1 = ((bf16[32,128,256]{2,1,0:T(8,128)(2,1)}), bf16[32,128,256]{2,1,0:T(8,128)(2,1)}, u32[]{:S(2)}, u32[]{:S(2)}) async-start(bf16[32,128,256]{2,1,0:T(8,128)(2,1)} %copy.44), calls=%async_computation.2 | async-start | bytes 4194304 | tf_op jit(solution)/shard_map/all_to_all | solution.py:48
  186.3 2.3 gather_fusion
  188.6 1.2 select_bitcast_fusion
  189.8 1.5 copy.41
  192.8 38.2 %all-gather.1 = f32[1024,128]{1,0:T(8,128)S(1)} all-gather(f32[64,128]{1,0:T(8,128)S(1)} %get-tuple-element.6), channel_id=3, replica_groups=mesh['dp'=32,'tensor'=16] {'tensor'}, dimensions={0}, use_global_device_ids=true | all-gather | bytes 557056 | tf_op jit(solution)/shard_map/all_gather | solution.py:8
  231.0 29.5 %all-gather.2 = f32[1024,128]{1,0:T(8,128)S(1)} all-gather(f32[64,128]{1,0:T(8,128)S(1)} %get-tuple-element.8), channel_id=4, replica_groups=mesh['dp'=32,'tensor'=16] {'tensor'}, dimensions={0}, use_global_device_ids=true | all-gather | bytes 557056 | tf_op jit(solution)/shard_map/all_gather | solution.py:8
  260.5 31.2 %all-gather.3 = f32[1024,128]{1,0:T(8,128)S(1)} all-gather(f32[64,128]{1,0:T(8,128)S(1)} %get-tuple-element.9), channel_id=5, replica_groups=mesh['dp'=32,'tensor'=16] {'tensor'}, dimensions={0}, use_global_device_ids=true | all-gather | bytes 557056 | tf_op jit(solution)/shard_map/all_gather | solution.py:8
  291.8 2.2 gather_fusion.1
  294.1 1.6 fusion.6
  295.7 1.6 fusion.7
  297.3 1.6 fusion.8
  298.9 0.7 pad_maximum_fusion
  (41 shorter events, 2.5 us)
Async XLA Ops:
  6.5 1.6 copy-start
  6.5 3.9 %copy-start.1 = (bf16[3,64,256]{2,1,0:T(8,128)(2,1)S(1)}, bf16[3,64,256]{2,1,0:T(8,128)(2,1)}, u32[]{:S(2)}) copy-start(bf16[3,64,256]{2,1,0:T(8,128)(2,1)} %param.11) | copy-start | bytes 294916
  6.5 287.5 %reduce-scatter.4.cloned.1.call-start = ((), (), s32[]{:S(2)}) async-start(), calls=%async_computation.5 | async-start | bytes 1114112 | tf_op jit(solution)/shard_map/reduce_scatter | solution.py:56
  10.4 1.6 copy-start.5
  10.4 1.6 copy-start.6
  10.4 110.5 %copy-start.2 = (bf16[4,256,128]{2,1,0:T(8,128)(2,1)S(1)}, bf16[4,256,128]{2,1,0:T(8,128)(2,1)}, u32[]{:S(2)}) copy-start(bf16[4,256,128]{2,1,0:T(8,128)(2,1)} %param.13) | copy-start | bytes 786436
  10.4 285.3 %reduce-scatter.6.cloned.1.call-start = ((), (), s32[]{:S(2)}) async-start(), calls=%async_computation.6 | async-start | bytes 1114112 | tf_op jit(solution)/shard_map/reduce_scatter | solution.py:56
  123.8 53.2 %all-to-all-start = ((bf16[32,256,128]{2,1,0:T(8,128)(2,1)}), bf16[32,256,128]{2,1,0:T(8,128)(2,1)}, u32[]{:S(2)}, u32[]{:S(2)}) async-start(bf16[32,256,128]{2,1,0:T(8,128)(2,1)} %copy.40), calls=%async_computation.1 | async-start | bytes 4194304 | tf_op jit(solution)/shard_map/all_to_all | solution.py:47
  151.5 1.6 copy-start.3
  151.5 145.8 %reduce-scatter.8.cloned.1.call-start = ((), (), s32[]{:S(2)}) async-start(), calls=%async_computation.7 | async-start | bytes 1114112 | tf_op jit(solution)/shard_map/reduce_scatter | solution.py:56
  156.4 29.8 %copy-start.4 = (s32[64]{0:T(128)S(1)}, s32[64]{0:T(128)}, u32[]{:S(2)}) copy-start(s32[64]{0:T(128)} %param.17) | copy-start | bytes 772
  177.1 114.7 %all-to-all-start.1 = ((bf16[32,128,256]{2,1,0:T(8,128)(2,1)}), bf16[32,128,256]{2,1,0:T(8,128)(2,1)}, u32[]{:S(2)}, u32[]{:S(2)}) async-start(bf16[32,128,256]{2,1,0:T(8,128)(2,1)} %copy.44), calls=%async_computation.2 | async-start | bytes 4194304 | tf_op jit(solution)/shard_map/all_to_all | solution.py:48
Sparse Core Ops, SparseCore 0:
  10.5 74.7 reduce-scatter.3
  88.3 68.1 reduce-scatter.5
  159.3 70.2 reduce-scatter.7
